TPU v7x, 32 devices: a whole 2x2x4 slice. The times are simulated.
32 devices in a mesh: row: 2 (over x), col: 8 (over z, y), layer: 2 (over core).
Axes of the slice: x: 2, y: 2, z: 4, core: 2. Of those that a mesh axis runs over, the one named last changes fastest.
Arguments:
- flow: float32 [2048, 2048], P('row', ('col', 'layer')), as said below
- pattern: int32 [4, 4], replicated, may hold values from 0 to 1, as said below
- prune_level: int32 [4], replicated, may hold values from 1 to 8
- power: int32 [4], replicated, may hold values from 1 to 4
Outputs:
- pruned: float32 [2048, 2048], P('row', ('col', 'layer'))
Inputs may be any that keep to these rules, and one draw needn't show every extreme that they name: pattern holds 0 or 1 and its diagonal is all 1; in every draw, all block rows that meet the 1024 rows of one index of row are all 1, and all block columns that meet the columns of one index of col are all 1. flow is positive.
All inputs are finite; a program needn't handle non-finite values.
Results may differ from a plain program's by a relative error of at most 0.00018.
Values sent between devices are 32-bit elements; how exact they have to be, the bound alone decides.
No kernel may reach another device: no remote copies, remote signals or barrier semaphores. Data moves between devices by JAX's collectives and lax.ppermute only.
A program may use at most 128 MiB of HBM per device.

v0:
```python
import jax
import jax.numpy as jnp
from jax import lax
from jax.sharding import PartitionSpec as P


def multiply(left, right):
    exact = lax.Precision.HIGHEST
    return jnp.dot(left, right, precision=exact, preferred_element_type=jnp.float32)


def on_device(flow, pattern, prune_level, power):
    rows, width = flow.shape
    layers = lax.axis_size("layer")
    order = rows * lax.axis_size("row")
    blocks = pattern.shape[0]
    tile_edge = order // blocks
    row_start = lax.axis_index("row") * rows
    col_start = (lax.axis_index("col") * layers + lax.axis_index("layer")) * width
    block_ids = jnp.arange(blocks, dtype=jnp.int32)
    row_ids = (row_start + jnp.arange(rows, dtype=jnp.int32)) // tile_edge
    col_ids = (col_start + jnp.arange(width, dtype=jnp.int32)) // tile_edge
    row_onehot = (row_ids[:, None] == block_ids[None, :]).astype(jnp.float32)
    col_onehot = (block_ids[:, None] == col_ids[None, :]).astype(jnp.float32)
    exact = lax.Precision.HIGHEST
    chosen = jnp.dot(
        jnp.dot(row_onehot, pattern.astype(jnp.float32), precision=exact),
        col_onehot,
        precision=exact,
    )
    masked = flow * chosen
    groups = rows // (layers * width)
    parted = masked.reshape(groups, layers, width, width)
    swapped = lax.all_to_all(parted, "layer", split_axis=1, concat_axis=3, tiled=True)
    inner_rows = swapped.reshape(groups * width, layers * width)
    strip = lax.all_gather(masked, "col", axis=1, tiled=True)
    partial_value = multiply(strip, lax.all_gather(inner_rows, "row", axis=0, tiled=True))
    expanded = lax.psum_scatter(partial_value, "layer", scatter_dimension=1, tiled=True)
    exponents = jnp.dot(power.astype(jnp.float32)[None, :], col_onehot, precision=exact)[0]
    inflated = jnp.power(expanded, exponents[None, :])
    totals = lax.psum(jnp.sum(inflated, axis=0), "row")
    levels = jnp.dot(prune_level.astype(jnp.float32)[None, :], col_onehot, precision=exact)[0] / 8.0
    return jnp.maximum(order * inflated / totals[None, :] - levels[None, :], 0.0)


def solution(mesh):
    return jax.shard_map(
        on_device,
        mesh=mesh,
        in_specs=(P("row", ("col", "layer")), P(), P(), P()),
        out_specs=P("row", ("col", "layer")),
        check_vma=False,
    )
```

profile of v0, /device:TPU:0, one launch (start us, length us, event | category | flops | bytes accessed | tf_op | source)
XLA Modules:
  0.0 145.4 jit_solution(2533182909635452199)
XLA Ops:
  6.5 0.0 all-gather.5.cloned.1.call-start
  6.6 1.1 fusion.1
  7.7 1.7 %convolution_multiply_fusion = f32[1024,128]{1,0:T(8,128)S(1)} fusion(f32[1024,128]{1,0:T(8,128)} %param.4, f32[1024,4]{0,1:T(4,128)S(1)} %fusion.1, s32[128]{0:T(128)S(1)} %and_select_fusion), kind=kOutput, calls=%fused_computation | convolution fusion | flops 6423040 | bytes 1065472 | tf_op jit(solution)/shard_map/dot_general | solution.py:26
  9.4 0.0 copy-start
  9.4 4.2 %all_to_all.15 = f32[4,2,128,128]{3,2,0,1:T(8,128)S(1)} all-to-all(f32[4,2,128,128]{3,2,0,1:T(8,128)S(1)} %copy.6), channel_id=1, replica_groups=mesh['row'=2,'col'=8,'layer'=2] {'layer'}, dimensions={1} | all-to-all | bytes 1048576 | tf_op jit(solution)/shard_map/all_to_all | solution.py:34
  13.6 0.4 copy.7
  14.0 0.9 copy.10
  14.8 0.0 copy-start.1
  14.8 0.0 copy-start.2
  14.9 0.0 all-gather.5.cloned.1.call-update
  14.9 0.0 all-gather.3.cloned.1.call-start
  14.9 0.0 copy-done
  14.9 0.7 all-gather.3.cloned.1.call-update
  15.6 0.0 reduce-scatter.2.cloned.1.call-start
  15.7 23.4 %all-gather.5.cloned.1.call-done = f32[1024,256]{1,0:T(8,128)} async-done(((f32[512,256]{1,0:T(8,128)}), f32[1024,256]{1,0:T(8,128)}) %all-gather.5.cloned.1.call-update) | async-done | bytes 1048592 | tf_op jit(solution)/shard_map/all_gather | solution.py:37
  39.0 77.1 %all-gather.3.cloned.1.call-done = f32[1024,1024]{1,0:T(8,128)} async-done(((f32[1024,128]{1,0:T(8,128)}), f32[1024,1024]{1,0:T(8,128)}) %all-gather.3.cloned.1.call-update) | async-done | bytes 4194320 | tf_op jit(solution)/shard_map/all_gather | solution.py:36
  116.1 6.9 %fusion.10 = f32[1024,256]{1,0:T(8,128)} fusion(f32[1024,1024]{1,0:T(8,128)} %all-gather.3.cloned.1.call-done, f32[1024,256]{1,0:T(8,128)} %all-gather.5.cloned.1.call-done), kind=kOutput, calls=%fused_computation.30 | convolution fusion | flops 3221225472 | bytes 6291456 | tf_op jit(solution)/shard_map/dot_general | solution.py:9
  123.0 0.0 reduce-scatter.2.cloned.1.call-update
  123.1 0.0 copy-done.1
  123.1 0.1 convolution_bitcast_fusion.1
  123.2 0.0 copy-done.2
  123.2 0.1 fusion
  123.3 6.6 %reduce-scatter.2.cloned.1.call-done = f32[1024,128]{1,0:T(8,128)} async-done(((f32[1024,256]{1,0:T(8,128)}), f32[1024,128]{1,0:T(8,128)}) %reduce-scatter.2.cloned.1.call-update) | async-done | bytes 524304 | tf_op jit(solution)/shard_map/reduce_scatter | solution.py:38
  129.9 1.6 %power_reduce_fusion = f32[128]{0:T(128)S(1)} fusion(f32[1024,128]{1,0:T(8,128)} %reduce-scatter.2.cloned.1.call-done, f32[128]{0:T(128)S(1)} %convolution_bitcast_fusion.1), kind=kLoop, calls=%fused_computation.8 | loop fusion | flops 130944 | bytes 525312 | tf_op jit(solution)/shard_map/reduce_sum | solution.py:41
  131.5 4.9 %psum.7 = f32[128]{0:T(128)S(1)} all-reduce(f32[128]{0:T(128)S(1)} %power_reduce_fusion), channel_id=1, replica_groups=mesh['row'=2,'col'=8,'layer'=2] {'row'}, use_global_device_ids=true, to_apply=%region_2.3 | all-reduce | flops 128 | bytes 1024 | tf_op jit(solution)/shard_map/psum | solution.py:41
  136.5 2.4 %subtract_maximum_fusion = f32[1024,128]{1,0:T(8,128)} fusion(f32[1024,128]{1,0:T(8,128)} %reduce-scatter.2.cloned.1.call-done, f32[128]{0:T(128)S(1)} %fusion, f32[128]{0:T(128)S(1)} %psum.7, f32[128]{0:T(128)S(1)} %convolution_bitcast_fusion.1), kind=kLoop, calls=%fused_computation.5 | loop fusion | flops 524288 | bytes 1050112 | tf_op jit(solution)/shard_map/max | solution.py:43
  (3 shorter events, 0.1 us)
Async XLA Ops:
  6.5 32.5 %all-gather.5.cloned.1.call-start = ((), (), s32[]{:S(2)}) async-start(), calls=%async_computation.3 | async-start | bytes 1572864 | tf_op jit(solution)/shard_map/all_gather | solution.py:37
  9.4 5.6 %copy-start = (f32[1024,128]{1,0:T(8,128)}, f32[1024,128]{1,0:T(8,128)S(1)}, u32[]{:S(2)}) copy-start(f32[1024,128]{1,0:T(8,128)S(1)} %convolution_multiply_fusion) | copy-start | bytes 1572868
  14.8 108.2 %copy-start.1 = (s32[4]{0:T(128)S(1)}, s32[4]{0:T(128)}, u32[]{:S(2)}) copy-start(s32[4]{0:T(128)} %param.7) | copy-start | bytes 52
  14.8 108.3 %copy-start.2 = (s32[4]{0:T(128)S(1)}, s32[4]{0:T(128)}, u32[]{:S(2)}) copy-start(s32[4]{0:T(128)} %param.6) | copy-start | bytes 52
  14.9 101.3 %all-gather.3.cloned.1.call-start = ((), (), s32[]{:S(2)}) async-start(), calls=%async_computation.2 | async-start | bytes 4718592 | tf_op jit(solution)/shard_map/all_gather | solution.py:36
  15.6 114.3 %reduce-scatter.2.cloned.1.call-start = ((), (), s32[]{:S(2)}) async-start(), calls=%async_computation.4 | async-start | bytes 1572864 | tf_op jit(solution)/shard_map/reduce_scatter | solution.py:38
Sparse Core Ops, SparseCore 0:
  15.0 23.9 all-gather.4
  41.1 75.0 all-gather.2
  123.2 6.7 reduce-scatter.1
where the time goes:
time: 146 us; the launch traced here: 145 us
  waiting for transfers between devices  108 us (74%)
  between operations  13.2 us (9%)
  matrix products  9.94 us (7%)
  blocking collectives  9.09 us (6%)
  other arithmetic  4.05 us (3%)
    all_gather x1, waiting for transfers between devices, on_device(): strip = lax.all_gather(masked, 'col', axis=1, tiled=True)  77.1 us
    all_gather x1, waiting for transfers between devices, on_device(): lax.all_gather(inner_rows, 'row', axis=0, tiled=True)  23.4 us
    dot_general x1, matrix products, multiply(): jnp.dot(left, right, precision=exact, preferred_element_type=jnp.float32)  6.9 us
    reduce_scatter x1, waiting for transfers between devices, on_device(): lax.psum_scatter(partial_value, 'layer', scatter_dimension=1, tiled=True)  6.61 us
    psum x1, blocking collectives, on_device(): totals = lax.psum(jnp.sum(inflated, axis=0), 'row')  4.94 us
    all_to_all x1, blocking collectives, on_device(): lax.all_to_all(parted, 'layer', split_axis=1, concat_axis=3, tiled=True)  4.15 us
  transfers between devices with their start and end apart: 3, of which 3 were waited for; matrix products, arithmetic and copies ran while one was open for 0% of the time, Pallas kernels for 0%

commit v1 on v0

--- a/solution.py
+++ b/solution.py
@@ -38,7 +38,7 @@
     expanded = lax.psum_scatter(partial_value, "layer", scatter_dimension=1, tiled=True)
     exponents = jnp.dot(power.astype(jnp.float32)[None, :], col_onehot, precision=exact)[0]
     inflated = jnp.power(expanded, exponents[None, :])
-    totals = lax.psum(jnp.sum(inflated, axis=0), "row")
+    totals = jnp.sum(lax.all_gather(jnp.sum(inflated, axis=0), "row"), axis=0)
     levels = jnp.dot(prune_level.astype(jnp.float32)[None, :], col_onehot, precision=exact)[0] / 8.0
     return jnp.maximum(order * inflated / totals[None, :] - levels[None, :], 0.0)
 

time: 146 us -> 145 us (level)
    psum x1 -> x0, blocking collectives: 4.94 us -> none  [on_device(): totals = lax.psum(jnp.sum(inflated, axis=0), 'row')]
    all_gather x0 -> x1, blocking collectives: none -> 4.21 us  [on_device(): totals = jnp.sum(lax.all_gather(jnp.sum(inflated, axis=0), 'row'), axis=0)]
where the time goes in v1:
time: 145 us
  waiting for transfers between devices  108 us (74%)
  between operations  13.2 us (9%)
  matrix products  9.94 us (7%)
  blocking collectives  8.37 us (6%)
  other arithmetic  4.07 us (3%)
    all_gather x1, waiting for transfers between devices, on_device(): strip = lax.all_gather(masked, 'col', axis=1, tiled=True)  77.1 us
    all_gather x1, waiting for transfers between devices, on_device(): lax.all_gather(inner_rows, 'row', axis=0, tiled=True)  23.4 us
    dot_general x1, matrix products, multiply(): jnp.dot(left, right, precision=exact, preferred_element_type=jnp.float32)  6.9 us
    reduce_scatter x1, waiting for transfers between devices, on_device(): lax.psum_scatter(partial_value, 'layer', scatter_dimension=1, tiled=True)  6.61 us
    all_gather x1, blocking collectives, on_device(): totals = jnp.sum(lax.all_gather(jnp.sum(inflated, axis=0), 'row'), axis=0)  4.21 us
    all_to_all x1, blocking collectives, on_device(): lax.all_to_all(parted, 'layer', split_axis=1, concat_axis=3, tiled=True)  4.15 us
  transfers between devices with their start and end apart: 3, of which 3 were waited for; matrix products, arithmetic and copies ran while one was open for 0% of the time, Pallas kernels for 0%

profile of v1, /device:TPU:0, one launch (start us, length us, event | category | flops | bytes accessed | tf_op | source)
XLA Modules:
  0.0 144.7 jit_solution(5760475188110092855)
XLA Ops:
  6.5 0.0 all-gather.7.cloned.1.call-start
  6.6 1.1 fusion.1
  7.7 1.7 %convolution_multiply_fusion = f32[1024,128]{1,0:T(8,128)S(1)} fusion(f32[1024,128]{1,0:T(8,128)} %param.4, f32[1024,4]{0,1:T(4,128)S(1)} %fusion.1, s32[128]{0:T(128)S(1)} %and_select_fusion), kind=kOutput, calls=%fused_computation | convolution fusion | flops 6423040 | bytes 1065472 | tf_op jit(solution)/shard_map/dot_general | solution.py:26
  9.4 0.0 copy-start
  9.4 4.2 %all_to_all.15 = f32[4,2,128,128]{3,2,0,1:T(8,128)S(1)} all-to-all(f32[4,2,128,128]{3,2,0,1:T(8,128)S(1)} %copy.6), channel_id=1, replica_groups=mesh['row'=2,'col'=8,'layer'=2] {'layer'}, dimensions={1} | all-to-all | bytes 1048576 | tf_op jit(solution)/shard_map/all_to_all | solution.py:34
  13.6 0.4 copy.7
  14.0 0.9 copy.10
  14.8 0.0 copy-start.1
  14.8 0.0 copy-start.2
  14.9 0.0 all-gather.7.cloned.1.call-update
  14.9 0.0 all-gather.5.cloned.1.call-start
  14.9 0.0 copy-done
  14.9 0.7 all-gather.5.cloned.1.call-update
  15.6 0.0 reduce-scatter.2.cloned.1.call-start
  15.7 23.4 %all-gather.7.cloned.1.call-done = f32[1024,256]{1,0:T(8,128)} async-done(((f32[512,256]{1,0:T(8,128)}), f32[1024,256]{1,0:T(8,128)}) %all-gather.7.cloned.1.call-update) | async-done | bytes 1048592 | tf_op jit(solution)/shard_map/all_gather | solution.py:37
  39.0 77.1 %all-gather.5.cloned.1.call-done = f32[1024,1024]{1,0:T(8,128)} async-done(((f32[1024,128]{1,0:T(8,128)}), f32[1024,1024]{1,0:T(8,128)}) %all-gather.5.cloned.1.call-update) | async-done | bytes 4194320 | tf_op jit(solution)/shard_map/all_gather | solution.py:36
  116.1 6.9 %fusion.10 = f32[1024,256]{1,0:T(8,128)} fusion(f32[1024,1024]{1,0:T(8,128)} %all-gather.5.cloned.1.call-done, f32[1024,256]{1,0:T(8,128)} %all-gather.7.cloned.1.call-done), kind=kOutput, calls=%fused_computation.30 | convolution fusion | flops 3221225472 | bytes 6291456 | tf_op jit(solution)/shard_map/dot_general | solution.py:9
  123.0 0.0 reduce-scatter.2.cloned.1.call-update
  123.1 0.0 copy-done.1
  123.1 0.1 convolution_bitcast_fusion.1
  123.2 0.0 copy-done.2
  123.2 0.1 fusion
  123.3 6.6 %reduce-scatter.2.cloned.1.call-done = f32[1024,128]{1,0:T(8,128)} async-done(((f32[1024,256]{1,0:T(8,128)}), f32[1024,128]{1,0:T(8,128)}) %reduce-scatter.2.cloned.1.call-update) | async-done | bytes 524304 | tf_op jit(solution)/shard_map/reduce_scatter | solution.py:38
  129.9 1.6 %power_reduce_fusion = f32[128]{0:T(128)S(1)} fusion(f32[1024,128]{1,0:T(8,128)} %reduce-scatter.2.cloned.1.call-done, f32[128]{0:T(128)S(1)} %convolution_bitcast_fusion.1), kind=kLoop, calls=%fused_computation.8 | loop fusion | flops 130944 | bytes 525312 | tf_op jit(solution)/shard_map/reduce_sum | solution.py:41
  131.5 4.2 %all-gather.1 = f32[2,1,128]{2,1,0:T(1,128)S(1)} all-gather(f32[1,1,128]{2,1,0:T(1,128)S(1)} %bitcast.30), channel_id=2, replica_groups=mesh['row'=2,'col'=8,'layer'=2] {'row'}, dimensions={0}, use_global_device_ids=true | all-gather | bytes 1536 | tf_op jit(solution)/shard_map/all_gather | solution.py:41
  135.8 2.4 %subtract_maximum_fusion = f32[1024,128]{1,0:T(8,128)} fusion(f32[1024,128]{1,0:T(8,128)} %reduce-scatter.2.cloned.1.call-done, f32[128]{0:T(128)S(1)} %fusion, f32[128]{0:T(128)S(1)} %reduce_sum.19, f32[128]{0:T(128)S(1)} %convolution_bitcast_fusion.1), kind=kLoop, calls=%fused_computation.5 | loop fusion | flops 524288 | bytes 1050112 | tf_op jit(solution)/shard_map/max | solution.py:43
  (4 shorter events, 0.1 us)
Async XLA Ops:
  6.5 32.5 %all-gather.7.cloned.1.call-start = ((), (), s32[]{:S(2)}) async-start(), calls=%async_computation.3 | async-start | bytes 1572864 | tf_op jit(solution)/shard_map/all_gather | solution.py:37
  9.4 5.6 %copy-start = (f32[1024,128]{1,0:T(8,128)}, f32[1024,128]{1,0:T(8,128)S(1)}, u32[]{:S(2)}) copy-start(f32[1024,128]{1,0:T(8,128)S(1)} %convolution_multiply_fusion) | copy-start | bytes 1572868
  14.8 108.2 %copy-start.1 = (s32[4]{0:T(128)S(1)}, s32[4]{0:T(128)}, u32[]{:S(2)}) copy-start(s32[4]{0:T(128)} %param.7) | copy-start | bytes 52
  14.8 108.3 %copy-start.2 = (s32[4]{0:T(128)S(1)}, s32[4]{0:T(128)}, u32[]{:S(2)}) copy-start(s32[4]{0:T(128)} %param.6) | copy-start | bytes 52
  14.9 101.3 %all-gather.5.cloned.1.call-start = ((), (), s32[]{:S(2)}) async-start(), calls=%async_computation.2 | async-start | bytes 4718592 | tf_op jit(solution)/shard_map/all_gather | solution.py:36
  15.6 114.3 %reduce-scatter.2.cloned.1.call-start = ((), (), s32[]{:S(2)}) async-start(), calls=%async_computation.4 | async-start | bytes 1572864 | tf_op jit(solution)/shard_map/reduce_scatter | solution.py:38
Sparse Core Ops, SparseCore 0:
  15.0 23.9 all-gather.6
  41.1 75.0 all-gather.4
  123.2 6.7 reduce-scatter.1

commit v2 on v0

--- a/solution.py
+++ b/solution.py
@@ -31,7 +31,10 @@
     masked = flow * chosen
     groups = rows // (layers * width)
     parted = masked.reshape(groups, layers, width, width)
-    swapped = lax.all_to_all(parted, "layer", split_axis=1, concat_axis=3, tiled=True)
+    swapped = jnp.concatenate(
+        lax.all_to_all(jnp.stack(jnp.split(parted, lax.axis_size("layer"), axis=1)), "layer", 0, 0),
+        axis=3,
+    )
     inner_rows = swapped.reshape(groups * width, layers * width)
     strip = lax.all_gather(masked, "col", axis=1, tiled=True)
     partial_value = multiply(strip, lax.all_gather(inner_rows, "row", axis=0, tiled=True))

time: 146 us -> 146 us (level)
  no operation moved by 1% of the time
where the time goes in v2:
time: 146 us; the launch traced here: 145 us
  waiting for transfers between devices  108 us (74%)
  between operations  13.2 us (9%)
  matrix products  9.95 us (7%)
  blocking collectives  9.09 us (6%)
  other arithmetic  4.09 us (3%)
    all_gather x1, waiting for transfers between devices, on_device(): strip = lax.all_gather(masked, 'col', axis=1, tiled=True)  77.1 us
    all_gather x1, waiting for transfers between devices, on_device(): lax.all_gather(inner_rows, 'row', axis=0, tiled=True)  23.4 us
    dot_general x1, matrix products, multiply(): jnp.dot(left, right, precision=exact, preferred_element_type=jnp.float32)  6.91 us
    reduce_scatter x1, waiting for transfers between devices, on_device(): lax.psum_scatter(partial_value, 'layer', scatter_dimension=1, tiled=True)  6.64 us
    psum x1, blocking collectives, on_device(): totals = lax.psum(jnp.sum(inflated, axis=0), 'row')  4.94 us
    all_to_all x1, blocking collectives, on_device(): lax.all_to_all(jnp.stack(jnp.split(parted, lax.axis_size('layer'), axis=1...  4.15 us
  transfers between devices with their start and end apart: 3, of which 3 were waited for; matrix products, arithmetic and copies ran while one was open for 0% of the time, Pallas kernels for 0%

profile of v2, /device:TPU:0, one launch (start us, length us, event | category | flops | bytes accessed | tf_op | source)
XLA Modules:
  0.0 145.5 jit_solution(1314343911504710024)
XLA Ops:
  6.5 0.0 all-gather.5.cloned.1.call-start
  6.6 1.1 fusion.1
  7.7 1.7 %convolution_multiply_fusion = f32[1024,128]{1,0:T(8,128)S(1)} fusion(f32[1024,128]{1,0:T(8,128)} %param.4, f32[1024,4]{0,1:T(4,128)S(1)} %fusion.1, s32[128]{0:T(128)S(1)} %and_select_fusion), kind=kOutput, calls=%fused_computation | convolution fusion | flops 6423040 | bytes 1065472 | tf_op jit(solution)/shard_map/dot_general | solution.py:26
  9.4 0.0 copy-start
  9.5 4.2 %all_to_all.5 = f32[2,4,1,128,128]{4,3,1,2,0:T(8,128)S(1)} all-to-all(f32[2,4,1,128,128]{4,3,1,2,0:T(8,128)S(1)} %pad_maximum_fusion), channel_id=1, replica_groups=mesh['row'=2,'col'=8,'layer'=2] {'layer'}, dimensions={0} | all-to-all | bytes 1048576 | tf_op jit(solution)/shard_map/all_to_all | solution.py:35
  13.6 0.4 copy.10
  14.0 0.8 copy.15
  14.9 0.0 copy-start.1
  14.9 0.0 copy-start.2
  14.9 0.0 all-gather.5.cloned.1.call-update
  14.9 0.0 all-gather.3.cloned.1.call-start
  15.0 0.0 copy-done
  15.0 0.7 all-gather.3.cloned.1.call-update
  15.7 0.0 reduce-scatter.2.cloned.1.call-start
  15.7 23.4 %all-gather.5.cloned.1.call-done = f32[1024,256]{1,0:T(8,128)} async-done(((f32[512,256]{1,0:T(8,128)}), f32[1024,256]{1,0:T(8,128)}) %all-gather.5.cloned.1.call-update) | async-done | bytes 1048592 | tf_op jit(solution)/shard_map/all_gather | solution.py:40
  39.1 77.1 %all-gather.3.cloned.1.call-done = f32[1024,1024]{1,0:T(8,128)} async-done(((f32[1024,128]{1,0:T(8,128)}), f32[1024,1024]{1,0:T(8,128)}) %all-gather.3.cloned.1.call-update) | async-done | bytes 4194320 | tf_op jit(solution)/shard_map/all_gather | solution.py:39
  116.2 6.9 %fusion.10 = f32[1024,256]{1,0:T(8,128)} fusion(f32[1024,1024]{1,0:T(8,128)} %all-gather.3.cloned.1.call-done, f32[1024,256]{1,0:T(8,128)} %all-gather.5.cloned.1.call-done), kind=kOutput, calls=%fused_computation.33 | convolution fusion | flops 3221225472 | bytes 6291456 | tf_op jit(solution)/shard_map/dot_general | solution.py:9
  123.1 0.0 reduce-scatter.2.cloned.1.call-update
  123.1 0.0 copy-done.1
  123.1 0.1 convolution_bitcast_fusion.1
  123.2 0.0 copy-done.2
  123.2 0.1 fusion
  123.4 6.6 %reduce-scatter.2.cloned.1.call-done = f32[1024,128]{1,0:T(8,128)} async-done(((f32[1024,256]{1,0:T(8,128)}), f32[1024,128]{1,0:T(8,128)}) %reduce-scatter.2.cloned.1.call-update) | async-done | bytes 524304 | tf_op jit(solution)/shard_map/reduce_scatter | solution.py:41
  130.0 1.6 %power_reduce_fusion = f32[128]{0:T(128)S(1)} fusion(f32[1024,128]{1,0:T(8,128)} %reduce-scatter.2.cloned.1.call-done, f32[128]{0:T(128)S(1)} %convolution_bitcast_fusion.1), kind=kLoop, calls=%fused_computation.9 | loop fusion | flops 130944 | bytes 525312 | tf_op jit(solution)/shard_map/reduce_sum | solution.py:44
  131.6 4.9 %psum.7 = f32[128]{0:T(128)S(1)} all-reduce(f32[128]{0:T(128)S(1)} %power_reduce_fusion), channel_id=1, replica_groups=mesh['row'=2,'col'=8,'layer'=2] {'row'}, use_global_device_ids=true, to_apply=%region_2.3 | all-reduce | flops 128 | bytes 1024 | tf_op jit(solution)/shard_map/psum | solution.py:44
  136.5 2.4 %subtract_maximum_fusion = f32[1024,128]{1,0:T(8,128)} fusion(f32[1024,128]{1,0:T(8,128)} %reduce-scatter.2.cloned.1.call-done, f32[128]{0:T(128)S(1)} %fusion, f32[128]{0:T(128)S(1)} %psum.7, f32[128]{0:T(128)S(1)} %convolution_bitcast_fusion.1), kind=kLoop, calls=%fused_computation.6 | loop fusion | flops 524288 | bytes 1050112 | tf_op jit(solution)/shard_map/max | solution.py:46
  (4 shorter events, 0.1 us)
Async XLA Ops:
  6.5 32.5 %all-gather.5.cloned.1.call-start = ((), (), s32[]{:S(2)}) async-start(), calls=%async_computation.3 | async-start | bytes 1572864 | tf_op jit(solution)/shard_map/all_gather | solution.py:40
  9.4 5.6 %copy-start = (f32[1024,128]{1,0:T(8,128)}, f32[1024,128]{1,0:T(8,128)S(1)}, u32[]{:S(2)}) copy-start(f32[1024,128]{1,0:T(8,128)S(1)} %convolution_multiply_fusion) | copy-start | bytes 1572868
  14.9 108.2 %copy-start.1 = (s32[4]{0:T(128)S(1)}, s32[4]{0:T(128)}, u32[]{:S(2)}) copy-start(s32[4]{0:T(128)} %param.7) | copy-start | bytes 52
  14.9 108.3 %copy-start.2 = (s32[4]{0:T(128)S(1)}, s32[4]{0:T(128)}, u32[]{:S(2)}) copy-start(s32[4]{0:T(128)} %param.6) | copy-start | bytes 52
  14.9 101.3 %all-gather.3.cloned.1.call-start = ((), (), s32[]{:S(2)}) async-start(), calls=%async_computation.2 | async-start | bytes 4718592 | tf_op jit(solution)/shard_map/all_gather | solution.py:39
  15.7 114.3 %reduce-scatter.2.cloned.1.call-start = ((), (), s32[]{:S(2)}) async-start(), calls=%async_computation.4 | async-start | bytes 1572864 | tf_op jit(solution)/shard_map/reduce_scatter | solution.py:41
Sparse Core Ops, SparseCore 0:
  15.0 23.9 all-gather.4
  41.1 75.0 all-gather.2
  123.2 6.7 reduce-scatter.1
